TPU v7x, 256 devices: a whole 4x4x8 slice. The times are simulated.
256 devices in a mesh: snp: 4 (over x), rows: 64 (over y, z, core).
Axes of the slice: x: 4, y: 4, z: 8, core: 2. Of those that a mesh axis runs over, the one named last changes fastest.
Arguments:
- genotypes: float32 [3072, 10240], P('snp', 'rows'), may hold values from -1 to 2, as said below
- relationship: float32 [10240, 10240], P('rows', 'snp'), as said below
Outputs:
- updated: float32 [10240, 10240], P('rows', 'snp')
- panel: float32 [10240, 512], P('rows')
Inputs may be any that keep to these rules, and one draw needn't show every extreme that they name: `genotypes`: expected count of the alternative allele, a real number between 0 and 2; exactly -1 marks a missing call. `relationship`: symmetric.
All inputs are finite; a program needn't handle non-finite values.
Results may differ from a plain program's by a relative error of at most 0.0007.
The roundings to bfloat16 on the way count: a program that leaves them out, or rounds other values in their place, can miss the bound.
Values may be sent and summed in bfloat16 or wider, within the bound.
A program may use at most 128 MiB of HBM per device.

v0:
```python
import jax
import jax.numpy as jnp
from jax import lax
from jax.sharding import PartitionSpec as P

PANEL = 512


RIDGE = 0.25


def from_root(x, axis, root):
    mine = lax.axis_index(axis) == root
    return lax.psum(jnp.where(mine, x, jnp.zeros_like(x)), axis)


def contract_snps(centered, shard_piece):
    return lax.dot_general(
        centered, shard_piece, (((0,), (0,)), ((), ())), preferred_element_type=jnp.float32
    )


def per_device(genotypes, relationship):
    ind_rows = genotypes.shape[1]
    width_cols = relationship.shape[1]
    called = genotypes >= 0
    dosage = jnp.where(called, genotypes, 0.0)
    totals, counts = lax.psum(
        (jnp.sum(dosage, axis=1), jnp.sum(called.astype(jnp.float32), axis=1)), "rows"
    )
    frequency = totals / (2.0 * counts)
    scale_total = lax.psum(jnp.sum(2.0 * frequency * (1.0 - frequency)), "snp")
    centered = jnp.where(called, dosage - 2.0 * frequency[:, None], 0.0).astype(jnp.bfloat16)
    partial_value = contract_snps(centered, lax.all_gather(centered, "rows", axis=1, tiled=True))
    summed = lax.psum_scatter(partial_value, "snp", scatter_dimension=1, tiled=True)
    rank_rows = lax.axis_index("rows")
    rank_snp = lax.axis_index("snp")
    row_ids = rank_rows * ind_rows + lax.broadcasted_iota(jnp.int32, (ind_rows, width_cols), 0)
    col_ids = rank_snp * width_cols + lax.broadcasted_iota(jnp.int32, (ind_rows, width_cols), 1)
    combined = relationship + summed / scale_total
    combined = combined + jnp.where(row_ids == col_ids, RIDGE, 0.0)
    block_count = (PANEL + ind_rows - 1) // ind_rows
    upper_blocks = []
    for root_block in range(block_count):
        upper_blocks.append(from_root(combined, "rows", root_block))
    upper_rows = jnp.concatenate(upper_blocks, axis=0)[:PANEL]
    diag_block, own_columns = (
        from_root(upper_rows[:, :PANEL], "snp", 0),
        from_root(combined[:, :PANEL], "snp", 0),
    )
    factor = jnp.linalg.cholesky(diag_block)
    own_panel = lax.linalg.triangular_solve(
        factor, own_columns, left_side=False, lower=True, transpose_a=True
    )
    column_panel = lax.linalg.triangular_solve(
        factor, upper_rows, left_side=True, lower=True, transpose_a=False
    )
    updated = combined - jnp.dot(own_panel, column_panel, precision=lax.Precision.HIGHEST)
    return (updated, own_panel)


def solution(mesh):
    placed = (P("snp", "rows"), P("rows", "snp"))
    return jax.shard_map(
        per_device,
        mesh=mesh,
        in_specs=placed,
        out_specs=(P("rows", "snp"), P("rows", None)),
        check_vma=False,
    )
```

profile of v0, /device:TPU:1, one launch (start us, length us, event | category | flops | bytes accessed | tf_op | source)
XLA Modules:
  0.0 806.7 jit_solution(17077195317906024965)
XLA Ops:
  8.3 130.3 %all-reduce.1 = (f32[768]{0:T(1024)S(1)}, f32[768]{0:T(1024)S(1)}) all-reduce(f32[768]{0:T(1024)S(1)} %get-tuple-element.17, f32[768]{0:T(1024)S(1)} %get-tuple-element.16), channel_id=1, replica_groups=mesh['snp'=4,'rows'=64] {'rows'}, use_global_device_ids=true, to_apply=%region_1.2 | all-reduce | flops 1536 | bytes 12288 | tf_op jit(solution)/shard_map/psum | solution.py:28
  141.1 95.8 %all-gather.2.cloned.1.call-done = bf16[768,10240]{0,1:T(8,128)(2,1)} async-done(((bf16[768,160]{0,1:T(8,128)(2,1)}), bf16[768,10240]{0,1:T(8,128)(2,1)}) %all-gather.2.cloned.1.call-update) | async-done | bytes 15728656 | tf_op jit(solution)/shard_map/all_gather | solution.py:34
  237.0 13.8 %fusion.67 = f32[160,10240]{0,1:T(8,128)} fusion(bf16[768,160]{0,1:T(8,128)(2,1)} %select_convert_fusion, bf16[768,10240]{0,1:T(8,128)(2,1)} %all-gather.2.cloned.1.call-done), kind=kOutput, calls=%fused_computation.122 | convolution fusion | flops 2516582400 | bytes 22528000 | tf_op jit(solution)/shard_map/dot_general | solution.py:18
  250.9 9.0 %psum.65 = f32[]{:T(128)} all-reduce(f32[]{:T(128)} %get-tuple-element.47), channel_id=1, replica_groups=mesh['snp'=4,'rows'=64] {'snp'}, use_global_device_ids=true, to_apply=%region_6.7 | all-reduce | flops 1 | bytes 8 | tf_op jit(solution)/shard_map/psum | solution.py:32
  261.9 85.7 %reduce-scatter.2.cloned.1.call-done = f32[160,2560]{0,1:T(8,128)} async-done(((f32[160,10240]{0,1:T(8,128)}), f32[160,2560]{0,1:T(8,128)}) %reduce-scatter.2.cloned.1.call-update) | async-done | bytes 1638416 | tf_op jit(solution)/shard_map/reduce_scatter | solution.py:35
  347.6 4.8 broadcast_select_fusion.3
  352.4 3.4 broadcast_select_fusion.2
  357.1 207.8 %all-reduce.7.cloned.1.call-done = (f32[160,2560]{0,1:T(8,128)}, f32[160,2560]{0,1:T(8,128)}, f32[160,2560]{0,1:T(8,128)}, f32[160,2560]{0,1:T(8,128)}) async-done(((f32[160,2560]{0,1:T(8,128)}, f32[160,2560]{0,1:T(8,128)}, f32[160,2560]{0,1:T(8,128)}, f32[160,2560]{0,1:T(8,128)}), (f32[160,2560]{0,1:T(8,128)}, f32[160,2560]{0,1:T(8,128)}, f32[160,2560]{0,1:T(8,128)}, ...) | async-done | bytes 6553616 | tf_op jit(solution)/shard_map/psum | solution.py:14
  564.9 2.9 fusion.25
  567.9 55.5 %all-reduce.9.cloned.1.call-done = (f32[160,512]{0,1:T(8,128)}, f32[512,512]{0,1:T(8,128)}) async-done(((f32[160,512]{0,1:T(8,128)}, f32[512,512]{0,1:T(8,128)}), (f32[160,512]{0,1:T(8,128)}, f32[512,512]{0,1:T(8,128)})) %all-reduce.9.cloned.1.call-update) | async-done | bytes 1376272 | tf_op jit(solution)/shard_map/psum | solution.py:14
  625.3 11.7 %cholesky.103 = f32[128,128]{1,0:T(8,128)S(1)} custom-call(f32[128,128]{1,0:T(8,128)S(1)} %cholesky.263), custom_call_target="Cholesky" | custom-call | tf_op jit(solution)/shard_map/jit(cholesky)/cholesky | solution.py:51
  637.1 9.8 %custom-call.32 = f32[1,128,128]{1,2,0:T(8,128)S(1)} custom-call(f32[1,128,128]{2,1,0:T(8,128)S(1)} %get-tuple-element.46), custom_call_target="InvertDiagBlocksLowerTriangular" | custom-call | tf_op jit(solution)/shard_map/jit(cholesky)/cholesky | solution.py:51
  647.6 11.7 %cholesky.215 = f32[128,128]{1,0:T(8,128)S(1)} custom-call(f32[128,128]{1,0:T(8,128)S(1)} %cholesky.267), custom_call_target="Cholesky" | custom-call | tf_op jit(solution)/shard_map/jit(cholesky)/cholesky | solution.py:51
  659.6 10.2 %custom-call.33 = f32[1,128,128]{1,2,0:T(8,128)S(1)} custom-call(f32[1,128,128]{2,1,0:T(8,128)S(1)} %get-tuple-element.44), custom_call_target="InvertDiagBlocksLowerTriangular" | custom-call | tf_op jit(solution)/shard_map/jit(cholesky)/cholesky | solution.py:51
  671.0 11.7 %cholesky.236 = f32[128,128]{1,0:T(8,128)S(1)} custom-call(f32[128,128]{1,0:T(8,128)S(1)} %cholesky.272), custom_call_target="Cholesky" | custom-call | tf_op jit(solution)/shard_map/jit(cholesky)/cholesky | solution.py:51
  682.9 9.8 %custom-call.34 = f32[1,128,128]{1,2,0:T(8,128)S(1)} custom-call(f32[1,128,128]{2,1,0:T(8,128)S(1)} %get-tuple-element.42), custom_call_target="InvertDiagBlocksLowerTriangular" | custom-call | tf_op jit(solution)/shard_map/jit(cholesky)/cholesky | solution.py:51
  693.5 11.9 %cholesky.253 = f32[128,128]{1,0:T(8,128)S(1)} custom-call(f32[128,128]{1,0:T(8,128)S(1)} %convolution_subtract_fusion.7), custom_call_target="Cholesky" | custom-call | tf_op jit(solution)/shard_map/jit(cholesky)/cholesky | solution.py:51
  711.0 11.8 %while.1 = (s32[]{:T(128)}, f32[512,512]{0,1:T(8,128)}, s32[4,2]{0,1:T(2,128)S(1)}, f32[4,128,128]{2,1,0:T(8,128)S(1)}, s32[]{:T(128)}) while((s32[]{:T(128)}, f32[512,512]{0,1:T(8,128)}, s32[4,2]{0,1:T(2,128)S(1)}, f32[4,128,128]{2,1,0:T(8,128)S(1)}, s32[]{:T(128)}) %tuple.34), condition=%wide.while_cond, body=%wide.while_body.sunk | while | flops 2 | bytes 393321 | solution.py:52
  722.8 39.3 %custom-call.35 = f32[4,128,128]{1,2,0:T(8,128)S(1)} custom-call(f32[4,128,128]{2,1,0:T(8,128)S(1)} %get-tuple-element.9), custom_call_target="InvertDiagBlocksLowerTriangular" | custom-call | tf_op jit(solution)/shard_map/triangular_solve | solution.py:52
  762.2 2.6 fusion.23
  764.8 3.9 convolution_subtract_fusion
  770.5 5.0 convolution_subtract_fusion.1
  777.2 7.4 fusion.17
  788.8 9.1 %fusion.8 = f32[160,2560]{0,1:T(8,128)S(1)} fusion(f32[160,2560]{0,1:T(8,128)S(1)} %copy-done.3, f32[160,512]{1,0:T(8,128)S(1)} %pad_maximum_fusion.6, f32[128,2560]{1,0:T(8,128)S(1)} %fusion.57, f32[128,2560]{1,0:T(8,128)S(1)} %fusion.55, f32[128,2560]{1,0:T(8,128)S(1)} %fusion.53, f32[128,2560]{1,0:T(8,128)S(1)} %fusion.23), kind=kOutput, calls=%fused_computation.10 | convolution fusion | flops 2520924160 | bytes 8847360 | tf_op jit(solution)/shard_map/dot_general | solution.py:58
  (99 shorter events, 36.2 us)
Async XLA Ops:
  7.2 229.8 %all-gather.2.cloned.1.call-start = ((), (), s32[]{:S(2)}) async-start(), calls=%async_computation.1 | async-start | bytes 15974400 | tf_op jit(solution)/shard_map/all_gather | solution.py:34
  141.1 206.6 %reduce-scatter.2.cloned.1.call-start = ((), (), s32[]{:S(2)}) async-start(), calls=%async_computation.2 | async-start | bytes 13107200 | tf_op jit(solution)/shard_map/reduce_scatter | solution.py:35
  250.8 9.1 %copy-start.7 = (f32[160,2560]{1,0:T(8,128)S(1)}, f32[160,2560]{1,0:T(8,128)}, u32[]{:S(2)}) copy-start(f32[160,2560]{1,0:T(8,128)} %param.3) | copy-start | bytes 4915204
  250.8 314.1 %all-reduce.7.cloned.1.call-start = ((), (), s32[]{:S(2)}) async-start(), calls=%async_computation.3 | async-start | bytes 20971520 | tf_op jit(solution)/shard_map/psum | solution.py:14
  352.4 3.9 copy-start.2
  355.8 267.6 %all-reduce.9.cloned.1.call-start = ((), (), s32[]{:S(2)}) async-start(), calls=%async_computation.4 | async-start | bytes 3145728 | tf_op jit(solution)/shard_map/psum | solution.py:14
  623.4 1.7 copy-start.6
  711.0 53.8 %copy-start = (f32[160,2560]{0,1:T(8,128)S(1)}, f32[160,2560]{0,1:T(8,128)}, u32[]{:S(2)}) copy-start(f32[160,2560]{0,1:T(8,128)} %get-tuple-element.30) | copy-start | bytes 4915204
  764.8 5.3 copy-start.5
  768.7 1.7 copy-start.1
  775.5 1.7 copy-start.4
  777.2 8.7 %copy-start.8 = (f32[160,512]{0,1:T(8,128)S(1)}, f32[160,512]{0,1:T(8,128)}, u32[]{:S(2)}) copy-start(f32[160,512]{0,1:T(8,128)} %get-tuple-element.32) | copy-start | bytes 983044
  784.7 4.1 copy-start.3
  788.8 9.2 %copy-start.9 = (f32[160,512]{1,0:T(8,128)}, f32[160,512]{1,0:T(8,128)S(1)}, u32[]{:S(2)}) copy-start(f32[160,512]{1,0:T(8,128)S(1)} %pad_maximum_fusion.6) | copy-start | bytes 983044
Sparse Core Ops, SparseCore 0:
  141.2 95.7 all-gather.1
  250.9 96.6 reduce-scatter.1
  355.9 208.9 all-reduce.6
  568.0 55.3 all-reduce.8
where the time goes:
time: 812 us; the launch traced here: 807 us
  waiting for transfers between devices  445 us (55%)
  blocking collectives  139 us (17%)
  other arithmetic  135 us (17%)
  matrix products  50.8 us (6%)
  local copies, waits for them, and re-layouts  19 us (2%)
  between operations  17.1 us (2%)
    psum x2, waiting for transfers between devices, from_root(): return lax.psum(jnp.where(mine, x, jnp.zeros_like(x)), axis)  263 us
    psum x1, blocking collectives, per_device(): lax.psum((jnp.sum(dosage, axis=1), jnp.sum(called.astype(jnp.float32), ax...  130 us
    all_gather x1, waiting for transfers between devices, per_device(): lax.all_gather(centered, 'rows', axis=1, tiled=True)  95.8 us
    reduce_scatter x1, waiting for transfers between devices, per_device(): lax.psum_scatter(partial_value, 'snp', scatter_dimension=1, tiled=True)  85.7 us
    another operation x14, other arithmetic, per_device(): factor = jnp.linalg.cholesky(diag_block)  79 us
    another operation x4, other arithmetic, per_device(): lax.linalg.triangular_solve(factor, own_columns, left_side=False, lower=T...  40.5 us
    another operation x7, matrix products, per_device(): lax.linalg.triangular_solve(factor, upper_rows, left_side=True, lower=Tru...  22.9 us
  transfers between devices with their start and end apart: 4, of which 4 were waited for; matrix products, arithmetic and copies ran while one was open for 0% of the time, Pallas kernels for 0%

commit v1 on v0

v1 whole, which is shorter than its diff:
```python
import jax
import jax.numpy as jnp
from jax import lax
from jax.experimental import pallas as pl
from jax.experimental.pallas import tpu as pltpu
from jax.sharding import PartitionSpec as P

PANEL = 512
RIDGE = 0.25
X, Y, Z, C = 4, 4, 8, 2
IND = 160
SNP = 768
WIDTH = 2560
COPIES = 240

HIGH = lax.Precision.HIGHEST
MESH = pl.DeviceIdType.MESH
F32 = jnp.float32
BF16 = jnp.bfloat16


def dot_tn(a, b, precision=HIGH):
    return lax.dot_general(a, b, (((0,), (0,)), ((), ())), precision=precision, preferred_element_type=F32)


def dot_nn(a, b, precision=HIGH):
    return lax.dot_general(a, b, (((1,), (0,)), ((), ())), precision=precision, preferred_element_type=F32)


def dot_nt(a, b, precision=None):
    return lax.dot_general(a, b, (((1,), (1,)), ((), ())), precision=precision, preferred_element_type=F32)


def three(x):
    high = x.astype(BF16)
    rest = x - high.astype(F32)
    mid = rest.astype(BF16)
    low = (rest - mid.astype(F32)).astype(BF16)
    return high.astype(F32), mid.astype(F32), low.astype(F32)


def outer_eight(a, b):
    ah, am, al = three(a)
    bh, bm, bl = three(b)
    left = jnp.concatenate([ah, ah, am, ah, al, am], 0).astype(BF16)
    right = jnp.concatenate([bh, bm, bh, bl, bh, bm], 0).astype(BF16)
    return dot_tn(left, right, None)


def eliminate_eight(row, inv, step):
    sub = lax.broadcasted_iota(jnp.int32, (8, 128), 0)
    cols = [jnp.broadcast_to(row[:, 8 * step + k : 8 * step + k + 1], (8, 128)) for k in range(8)]
    for j in range(8):
        root = lax.rsqrt(cols[j][j : j + 1, :])
        mult = jnp.where(sub > j, cols[j] * root, 0.0)
        row_j = row[j : j + 1, :] * root
        inv_j = inv[j : j + 1, :] * root
        row = jnp.where(sub == j, row_j, row - mult * row_j)
        inv = jnp.where(sub == j, inv_j, inv - mult * inv_j)
        for k in range(j + 1, 8):
            cols[k] = cols[k] - mult * (cols[k][j : j + 1, :] * root)
    return row, inv


def factor_block(d_ref):
    for step in range(16):
        lo = 8 * step
        row, inv = eliminate_eight(d_ref[lo : lo + 8, 0:128], d_ref[lo : lo + 8, 128:256], step)
        d_ref[lo : lo + 8, 0:128] = row
        d_ref[lo : lo + 8, 128:256] = inv
        if step < 15:
            prod = outer_eight(row, jnp.concatenate([row, inv], 1))
            d_ref[lo + 8 : 128, :] = d_ref[lo + 8 : 128, :] - prod[lo + 8 : 128, :]


def cholesky_part(b, a_ref, x_ref, d_ref):
    i0 = lax.broadcasted_iota(jnp.int32, (128, 128), 0)
    i1 = lax.broadcasted_iota(jnp.int32, (128, 128), 1)
    lo, hi = 128 * b, 128 * b + 128
    d_ref[:, 0:128] = a_ref[lo:hi, lo:hi]
    d_ref[:, 128:256] = jnp.where(i0 == i1, 1.0, 0.0).astype(F32)
    factor_block(d_ref)
    xd = d_ref[:, 128:256]
    x_row = dot_nn(xd, x_ref[lo:hi, 0:hi])
    x_ref[lo:hi, 0:hi] = x_row
    if hi < PANEL:
        right = dot_nn(xd, a_ref[lo:hi, hi:PANEL])
        a_ref[hi:PANEL, hi:PANEL] = a_ref[hi:PANEL, hi:PANEL] - dot_tn(right, right)
        x_ref[hi:PANEL, 0:hi] = x_ref[hi:PANEL, 0:hi] - dot_tn(right, x_row)


def kernel(
    gen, rel, out, panel,
    sum_a, sum_b, scale_buf, rel_piece, own_rows, cols, top, top_rel,
    part_a, recv_a, a11, part_u, recv_u, a21, upper, amat, xmat, dmat, comb_t, wmat,
    send_sem, recv_sem,
):
    x = lax.axis_index("snp")
    r = lax.axis_index("rows")
    y, z, c = r // 16, (r // 2) % 8, r % 2
    k_own = 2 * z + c
    count = [0]
    unsent = []

    def device(xx, yy, zz, cc):
        return (xx, yy * 16 + zz * 2 + cc)

    def x_peer(d):
        return device((x + d) % X, y, z, c)

    def y_peer(d):
        return device(x, (y + d) % Y, z, c)

    def z_peer(d):
        return device(x, y, (z + d) % Z, c)

    sibling = device(x, y, z, 1 - c)
    mirror = device(y, x, z, c)

    def slots(n):
        first = count[0]
        count[0] += n
        return first

    def describe(src, dst, to, slot):
        return pltpu.make_async_remote_copy(
            src_ref=src, dst_ref=dst, send_sem=send_sem.at[slot], recv_sem=recv_sem.at[slot],
            device_id=to, device_id_type=MESH,
        )

    def send(src, dst, to):
        copy = describe(src, dst, to, slots(1))
        copy.start()
        unsent.append((None, copy))
        return copy

    def send_if(cond, src, dst, to):
        copy = describe(src, dst, to, slots(1))
        pl.when(cond)(copy.start)
        unsent.append((cond, copy))
        return copy

    def arrive(copies):
        for copy in copies:
            copy.wait_recv()

    barrier = pltpu.get_barrier_semaphore()
    greeted = [x_peer(d) for d in range(1, X)]
    greeted += [device(x, (y + d) % Y, z, (c + e) % C) for d in range(Y) for e in range(C) if d or e]
    greeted += [z_peer(d) for d in range(1, Z)]
    for to in greeted:
        pl.semaphore_signal(barrier, inc=1, device_id=to, device_id_type=MESH)

    @pl.when(x != y)
    def _():
        pl.semaphore_signal(barrier, inc=1, device_id=mirror, device_id_type=MESH)
        pl.semaphore_wait(barrier, len(greeted) + 1)

    @pl.when(x == y)
    def _():
        pl.semaphore_wait(barrier, len(greeted))

    rel_copies = []
    rel_slot = slots(1)
    rel_send = slots(3)
    for d in range(1, X):
        copy = pltpu.make_async_remote_copy(
            src_ref=rel.at[:, 128 * d : 128 * d + 128], dst_ref=rel_piece,
            send_sem=send_sem.at[rel_send + d - 1], recv_sem=recv_sem.at[rel_slot],
            device_id=device(d, y, z, c), device_id_type=MESH,
        )
        rel_copies.append(copy)

    @pl.when(x == 0)
    def _():
        for copy in rel_copies:
            copy.start()
        rel_piece[...] = rel[:, 0:128]

    for copy in rel_copies:
        unsent.append((x == 0, copy))

    values = gen[...]
    called = values >= 0
    dosage = jnp.where(called, values, 0.0)
    sums = jnp.concatenate(
        [jnp.sum(dosage, axis=0, keepdims=True), jnp.sum(called.astype(F32), axis=0, keepdims=True)], 0
    )
    yc = 2 * y + c
    sum_a[yc] = sums
    copies = [
        send(sum_a.at[yc], sum_a.at[yc], device(x, (y + d) % Y, z, (c + e) % C))
        for d in range(Y) for e in range(C) if d or e
    ]
    arrive(copies)
    sum_b[z] = jnp.sum(sum_a[...], axis=0)
    copies = [send(sum_b.at[z], sum_b.at[z], z_peer(d)) for d in range(1, Z)]
    arrive(copies)
    both = jnp.sum(sum_b[...], axis=0)
    frequency = both[0:1, :] / (2.0 * both[1:2, :])
    scale_part = jnp.sum(2.0 * frequency * (1.0 - frequency))
    scale_buf[x] = jnp.full((8, 128), scale_part, F32)
    scale_copies = [send(scale_buf.at[x], scale_buf.at[x], x_peer(d)) for d in range(1, X)]
    own_rows[x] = jnp.where(called, dosage - 2.0 * frequency, 0.0).astype(BF16)

    @pl.when(x != 0)
    def _():
        rel_copies[0].wait_recv()

    def top_at(k, q):
        rows = pl.ds(pl.multiple_of(k * IND + 80 * (q // 2), 16), 80)
        lanes = pl.ds(pl.multiple_of(384 * (q % 2), 128), 384)
        return top.at[rows, lanes]

    def top_rel_at(k, q):
        return top_rel.at[pl.ds(pl.multiple_of(k * IND + 40 * q, 8), 40)]

    first_slot = slots(2)
    source = jnp.logical_and(y == 0, z < 2)
    to_send = []
    for d in range(1, Y):
        rows, lanes = pl.ds(80 * (d // 2), 80), pl.ds(384 * (d % 2), 384)
        send_slot = slots(2)
        for i, (src, dst) in enumerate((
            (own_rows.at[x, rows, lanes], top_at(k_own, d)),
            (rel_piece.at[pl.ds(40 * d, 40)], top_rel_at(k_own, d)),
        )):
            to_send.append(pltpu.make_async_remote_copy(
                src_ref=src, dst_ref=dst, send_sem=send_sem.at[send_slot + i], recv_sem=recv_sem.at[first_slot + i],
                device_id=device(x, d, z, c), device_id_type=MESH,
            ))

    @pl.when(source)
    def _():
        for copy in to_send:
            copy.start()
        top[pl.ds(pl.multiple_of(k_own * IND, 16), 80), 0:384] = own_rows[x, 0:80, 0:384]
        top_rel[pl.ds(pl.multiple_of(k_own * IND, 8), 40)] = rel_piece[0:40]

    for copy in to_send:
        unsent.append((source, copy))

    def col_at(a, k, part):
        return cols.at[a, pl.ds(pl.multiple_of(k * IND, 16), IND), pl.ds(384 * part, 384)]

    def up_at(a, k, part):
        return upper.at[a, pl.ds(pl.multiple_of(k * IND + 80 * part, 8), 80)]

    own_slice = pl.ds(pl.multiple_of(k_own * IND, 16), IND)
    swap = send_if(x != y, own_rows.at[x], cols.at[x, own_slice], mirror)

    @pl.when(x == y)
    def _():
        cols[x, own_slice] = own_rows[x]

    row_copies = [send(own_rows.at[x], own_rows.at[x], x_peer(d)) for d in range(1, X)]

    @pl.when(jnp.logical_and(y != 0, z < 2))
    def _():
        for copy in to_send[:2]:
            copy.wait_recv()

    z_slot = slots(4)
    z_copies = []
    for d in range(1, Z):
        send_slot = slots(2)
        for i, ref in enumerate((top_at(k_own, y), top_rel_at(k_own, y))):
            z_copies.append(pltpu.make_async_remote_copy(
                src_ref=ref, dst_ref=ref, send_sem=send_sem.at[send_slot + i],
                recv_sem=recv_sem.at[z_slot + 2 * (z % 2) + i], device_id=z_peer(d), device_id_type=MESH,
            ))

    @pl.when(z < 2)
    def _():
        for copy in z_copies:
            copy.start()

    for copy in z_copies:
        unsent.append((z < 2, copy))

    def plane_gather(at):
        every = slice(None)
        across = [send(at(y, k_own, 0), at(y, k_own, 0), y_peer(d)) for d in range(1, Y)]

        def ring(k_plus, k_minus, a, part, plus, minus):
            made = []
            if plus:
                made.append(send(at(a, k_plus, part), at(a, k_plus, part), z_peer(1)))
            if minus:
                made.append(send(at(a, k_minus, part), at(a, k_minus, part), z_peer(Z - 1)))
            return made

        ring_two = ring(k_own, k_own, y, 1, True, True)
        spread = [send(at(y, k_own, 1), at(y, k_own, 1), y_peer(d)) for d in range(1, Y)]
        yield
        arrive(across)
        ring_one = ring(k_own, k_own, every, 0, True, True)
        passed = [send(at(every, k_own, 0), at(every, k_own, 0), sibling)]
        spread_ks = [k_own]
        yield
        for t in range(1, 5):
            k_minus = 2 * ((z + t) % Z) + c
            k_plus = 2 * ((z + Z - t) % Z) + c
            ks = [k_plus, k_minus] if t < 4 else [k_plus]
            arrive(ring_two)
            if t < 4:
                ring_two = ring(k_plus, k_minus, y, 1, True, t < 3)
            later = [send(at(y, k, 1), at(y, k, 1), y_peer(d)) for k in ks for d in range(1, Y)]
            arrive(ring_one)
            if t < 4:
                ring_one = ring(k_plus, k_minus, every, 0, True, t < 3)
            passed += [send(at(every, k, 0), at(every, k, 0), sibling) for k in ks]
            arrive(spread)
            passed += [send(at(every, k, 1), at(every, k, 1), sibling) for k in spread_ks]
            spread, spread_ks = later, ks
            yield
        arrive(spread)
        passed += [send(at(every, k, 1), at(every, k, 1), sibling) for k in spread_ks]
        yield
        arrive(passed)
        yield

    @pl.when(x != y)
    def _():
        swap.wait_recv()

    gather = plane_gather(col_at)
    next(gather)

    for zs in range(2):
        @pl.when(z != zs)
        def _(zs=zs):
            for i, ref in enumerate((top_at(2 * zs + c, y), top_rel_at(2 * zs + c, y))):
                describe(ref, ref, z_peer(1), z_slot + 2 * zs + i).wait_recv()

    copies = [
        send(ref, ref, y_peer(d))
        for d in range(1, Y) for zs in range(2) for ref in (top_at(2 * zs + c, y), top_rel_at(2 * zs + c, y))
    ]
    next(gather)
    arrive(copies)
    whole = [pl.ds(pl.multiple_of((2 * zs + c) * IND, 16), IND) for zs in range(2)]
    copies = [send(ref.at[s], ref.at[s], sibling) for s in whole for ref in (top, top_rel)]
    arrive(copies)

    for xx in range(X):
        part_a[xx] = dot_nt(top[0:PANEL, :], top[128 * xx : 128 * xx + 128, :])
        part_u[xx] = dot_nt(own_rows[x], top[128 * xx : 128 * xx + 128, :])
    half = pl.ds(pl.multiple_of(256 * c, 8), 256)
    a_copies = [send(part_a.at[(x + d) % X, half], recv_a.at[d - 1], x_peer(d)) for d in range(1, X)]
    u_copies = [send(part_u.at[(x + d) % X], recv_u.at[d - 1], x_peer(d)) for d in range(1, X)]
    arrive(scale_copies)
    scale = 1.0 / (scale_buf[0] + scale_buf[1] + scale_buf[2] + scale_buf[3])[0:1, 0:1]

    next(gather)
    arrive(a_copies)
    lane = 128 * x + lax.broadcasted_iota(jnp.int32, (256, 128), 1)
    row = 256 * c + lax.broadcasted_iota(jnp.int32, (256, 128), 0)
    total = part_a[x, half] + recv_a[0] + recv_a[1] + recv_a[2]
    a11[x, half] = top_rel[half] + total * scale + jnp.where(lane == row, RIDGE, 0.0)
    a_copies = [send(a11.at[x, half], a11.at[x, half], x_peer(d)) for d in range(1, X)]
    arrive(u_copies)
    lane = 128 * x + lax.broadcasted_iota(jnp.int32, (IND, 128), 1)
    row = IND * r + lax.broadcasted_iota(jnp.int32, (IND, 128), 0)
    total = part_u[x] + recv_u[0] + recv_u[1] + recv_u[2]
    mine = rel_piece[...] + total * scale + jnp.where(lane == row, RIDGE, 0.0)
    a21[x] = mine
    u_swap = send_if(x != y, a21.at[x], upper.at[x, own_slice], mirror)

    @pl.when(x == y)
    def _():
        upper[x, own_slice] = mine

    u_copies = [send(a21.at[x], a21.at[x], x_peer(d)) for d in range(1, X)]
    arrive(a_copies)
    a_copy = send(a11.at[:, half], a11.at[:, half], sibling)
    next(gather)
    a_copy.wait_recv()
    for xx in range(X):
        amat[:, 128 * xx : 128 * xx + 128] = a11[xx]
    i0 = lax.broadcasted_iota(jnp.int32, (PANEL, PANEL), 0)
    i1 = lax.broadcasted_iota(jnp.int32, (PANEL, PANEL), 1)
    xmat[...] = jnp.where(i0 == i1, 1.0, 0.0).astype(F32)
    cholesky_part(0, amat, xmat, dmat)
    next(gather)
    cholesky_part(1, amat, xmat, dmat)
    next(gather)

    @pl.when(x != y)
    def _():
        u_swap.wait_recv()

    u_gather = plane_gather(up_at)
    next(u_gather)
    next(gather)
    cholesky_part(2, amat, xmat, dmat)
    next(u_gather)
    next(gather)
    next(u_gather)
    cholesky_part(3, amat, xmat, dmat)
    arrive(u_copies)
    own = jnp.concatenate([a21[0], a21[1], a21[2], a21[3]], 1)
    own_panel = dot_nt(own, xmat[...], HIGH)
    panel[...] = own_panel
    wmat[...] = dot_nn(own_panel, xmat[...])
    next(u_gather)

    arrive(row_copies)

    def gram_part(i, carry):
        rows = pl.ds(pl.multiple_of(i * 256, 16), 256)
        total = dot_nt(cols[0, rows], own_rows[0])
        for a in range(1, X):
            total = total + dot_nt(cols[a, rows], own_rows[a])
        comb_t[rows, :] = total * scale
        return carry

    lax.fori_loop(0, 5, gram_part, 0)
    next(u_gather)
    lax.fori_loop(5, 10, gram_part, 0)
    next(u_gather)
    next(u_gather)
    next(u_gather)

    def last_part(i, carry):
        rows = pl.ds(pl.multiple_of(i * 256, 16), 256)
        up = jnp.concatenate([upper[0, rows], upper[1, rows], upper[2, rows], upper[3, rows]], 1)
        comb_t[rows, :] = comb_t[rows, :] - dot_nt(up, wmat[...], HIGH)
        return carry

    lax.fori_loop(0, 10, last_part, 0)
    for i in range(WIDTH // 128):
        lanes = slice(128 * i, 128 * i + 128)
        lane = WIDTH * x + 128 * i + lax.broadcasted_iota(jnp.int32, (IND, 128), 1)
        out[:, lanes] = rel[:, lanes] + comb_t[lanes, :].T + jnp.where(lane == row, RIDGE, 0.0)

    for cond, copy in unsent:
        if cond is None:
            copy.wait_send()
        else:
            pl.when(cond)(copy.wait_send)
    assert count[0] <= COPIES, count[0]


def per_device(genotypes, relationship):
    vmem = pl.BlockSpec(memory_space=pltpu.VMEM)
    return pl.pallas_call(
        kernel,
        out_shape=(
            jax.ShapeDtypeStruct((IND, WIDTH), F32),
            jax.ShapeDtypeStruct((IND, PANEL), F32),
        ),
        in_specs=[vmem, vmem],
        out_specs=(vmem, vmem),
        scratch_shapes=[
            pltpu.VMEM((8, 2, SNP), F32),
            pltpu.VMEM((8, 2, SNP), F32),
            pltpu.VMEM((X, 8, 128), F32),
            pltpu.VMEM((IND, 128), F32),
            pltpu.VMEM((X, IND, SNP), BF16),
            pltpu.VMEM((X, WIDTH, SNP), BF16),
            pltpu.VMEM((640, SNP), BF16),
            pltpu.VMEM((640, 128), F32),
            pltpu.VMEM((X, PANEL, 128), F32),
            pltpu.VMEM((3, 256, 128), F32),
            pltpu.VMEM((X, PANEL, 128), F32),
            pltpu.VMEM((X, IND, 128), F32),
            pltpu.VMEM((3, IND, 128), F32),
            pltpu.VMEM((X, IND, 128), F32),
            pltpu.VMEM((X, WIDTH, 128), F32),
            pltpu.VMEM((PANEL, PANEL), F32),
            pltpu.VMEM((PANEL, PANEL), F32),
            pltpu.VMEM((128, 256), F32),
            pltpu.VMEM((WIDTH, IND), F32),
            pltpu.VMEM((IND, PANEL), F32),
            pltpu.SemaphoreType.DMA((COPIES,)),
            pltpu.SemaphoreType.DMA((COPIES,)),
        ],
        compiler_params=pltpu.CompilerParams(
            collective_id=0, has_side_effects=True, vmem_limit_bytes=56 * 1024 * 1024
        ),
        name="update",
    )(genotypes.T, relationship)


def solution(mesh):
    return jax.shard_map(
        per_device,
        mesh=mesh,
        in_specs=(P("snp", "rows"), P("rows", "snp")),
        out_specs=(P("rows", "snp"), P("rows", None)),
        check_vma=False,
    )
```

time: 812 us -> 159 us (0.20)
  waiting for transfers between devices: 445 us -> 0 us
  Pallas kernels: 0 us -> 155 us
  blocking collectives: 139 us -> 0 us
  other arithmetic: 135 us -> 0 us
  matrix products: 50.8 us -> 0 us
  between operations: 17.1 us -> 0.65 us
  local copies, waits for them, and re-layouts: 19 us -> 3.48 us
    psum x2 -> x0, waiting for transfers between devices: 263 us -> none  [from_root(): return lax.psum(jnp.where(mine, x, jnp.zeros_like(x)), axis)]
    pallas_call x0 -> x1, Pallas kernels: none -> 155 us  [per_device(): pl.pallas_call(kernel, out_shape=(jax.ShapeDtypeStruct((IND, WIDTH), F32)...]
    psum x2 -> x0, blocking collectives: 139 us -> none  [the longest x1 130 us: per_device(): lax.psum((jnp.sum(dosage, axis=1), jnp.sum(called.astype(jnp.float32), ax...]
    another operation x18 -> x0, other arithmetic: 119 us -> none  [the longest x14 79 us: per_device(): factor = jnp.linalg.cholesky(diag_block)]
    all_gather x1 -> x0, waiting for transfers between devices: 95.8 us -> none  [per_device(): lax.all_gather(centered, 'rows', axis=1, tiled=True)]
    reduce_scatter x1 -> x0, waiting for transfers between devices: 85.7 us -> none  [per_device(): lax.psum_scatter(partial_value, 'snp', scatter_dimension=1, tiled=True)]
    another operation x20 -> x0, matrix products: 27.9 us -> none  [the longest x7 22.9 us: per_device(): lax.linalg.triangular_solve(factor, upper_rows, left_side=True, lower=Tru...]
    dot_general x2 -> x0, matrix products: 23 us -> none  [the longest x1 13.8 us: contract_snps(): lax.dot_general(centered, shard_piece, (((0,), (0,)), ((), ())), preferre...]
  transfers between devices with their start and end apart: 4 -> 0, of which waited for: 4 -> 0; matrix products, arithmetic and copies ran while one was open for 0% -> 0% of each run, Pallas kernels for 0% -> 0%
where the time goes in v1:
time: 159 us
  Pallas kernels  155 us (97%)
  local copies, waits for them, and re-layouts  3.48 us (2%)
    pallas_call x1, Pallas kernels, per_device(): pl.pallas_call(kernel, out_shape=(jax.ShapeDtypeStruct((IND, WIDTH), F32)...  155 us
    unnamed x4, local copies, waits for them, and re-layouts  3.48 us

profile of v1, /device:TPU:1, one launch (start us, length us, event | category | flops | bytes accessed | tf_op | source)
XLA Modules:
  0.0 158.7 jit_solution(6010917437522635674)
XLA Ops:
  0.6 154.5 %update.1 = (f32[160,2560]{1,0:T(8,128)}, f32[160,512]{1,0:T(8,128)}) custom-call(f32[160,768]{1,0:T(8,128)} %bitcast.1, f32[160,2560]{1,0:T(8,128)} %rel.1), custom_call_target="tpu_custom_call" | custom-call | tf_op jit(solution)/shard_map/update/pallas_call | solution.py:447
  155.2 0.0 copy-start
  155.2 2.8 %copy.6 = f32[160,2560]{1,0:T(8,128)} copy(f32[160,2560]{1,0:T(8,128)} %get-tuple-element.4) | data formatting | bytes 3276800
  157.9 0.0 copy-done
  157.9 0.7 copy.7
Async XLA Ops:
  155.2 2.8 %copy-start = (f32[160,512]{1,0:T(8,128)S(1)}, f32[160,512]{1,0:T(8,128)}, u32[]{:S(2)}) copy-start(f32[160,512]{1,0:T(8,128)} %get-tuple-element.5) | copy-start | bytes 983044

commit v2 on v1

v2 whole, which is shorter than its diff:
```python
import jax
import jax.numpy as jnp
from jax import lax
from jax.experimental import pallas as pl
from jax.experimental.pallas import tpu as pltpu
from jax.sharding import PartitionSpec as P

PANEL = 512
RIDGE = 0.25
X, Y, Z, C = 4, 4, 8, 2
IND = 160
SNP = 768
WIDTH = 2560
COPIES = 320

HIGH = lax.Precision.HIGHEST
MESH = pl.DeviceIdType.MESH
F32 = jnp.float32
BF16 = jnp.bfloat16


def dot_tn(a, b, precision=HIGH):
    return lax.dot_general(a, b, (((0,), (0,)), ((), ())), precision=precision, preferred_element_type=F32)


def dot_nn(a, b, precision=HIGH):
    return lax.dot_general(a, b, (((1,), (0,)), ((), ())), precision=precision, preferred_element_type=F32)


def dot_nt(a, b, precision=None):
    return lax.dot_general(a, b, (((1,), (1,)), ((), ())), precision=precision, preferred_element_type=F32)


def three(x):
    high = x.astype(BF16)
    rest = x - high.astype(F32)
    mid = rest.astype(BF16)
    low = (rest - mid.astype(F32)).astype(BF16)
    return high.astype(F32), mid.astype(F32), low.astype(F32)


def outer_eight(a, b):
    ah, am, al = three(a)
    bh, bm, bl = three(b)
    left = jnp.concatenate([ah, ah, am, ah, al, am], 0).astype(BF16)
    right = jnp.concatenate([bh, bm, bh, bl, bh, bm], 0).astype(BF16)
    return dot_tn(left, right, None)


def eliminate_eight(row, inv, step):
    sub = lax.broadcasted_iota(jnp.int32, (8, 128), 0)
    cols = [jnp.broadcast_to(row[:, 8 * step + k : 8 * step + k + 1], (8, 128)) for k in range(8)]
    for j in range(8):
        root = lax.rsqrt(cols[j][j : j + 1, :])
        mult = jnp.where(sub > j, cols[j] * root, 0.0)
        row_j = row[j : j + 1, :] * root
        inv_j = inv[j : j + 1, :] * root
        row = jnp.where(sub == j, row_j, row - mult * row_j)
        inv = jnp.where(sub == j, inv_j, inv - mult * inv_j)
        for k in range(j + 1, 8):
            cols[k] = cols[k] - mult * (cols[k][j : j + 1, :] * root)
    return row, inv


def factor_steps(d_ref, first, last):
    for step in range(first, last):
        lo = 8 * step
        row, inv = eliminate_eight(d_ref[lo : lo + 8, 0:128], d_ref[lo : lo + 8, 128:256], step)
        d_ref[lo : lo + 8, 0:128] = row
        d_ref[lo : lo + 8, 128:256] = inv
        if step < 15:
            prod = outer_eight(row, jnp.concatenate([row, inv], 1))
            d_ref[lo + 8 : 128, :] = d_ref[lo + 8 : 128, :] - prod[lo + 8 : 128, :]


def cholesky_first(b, a_ref, d_ref):
    i0 = lax.broadcasted_iota(jnp.int32, (128, 128), 0)
    i1 = lax.broadcasted_iota(jnp.int32, (128, 128), 1)
    lo, hi = 128 * b, 128 * b + 128
    d_ref[:, 0:128] = a_ref[lo:hi, lo:hi]
    d_ref[:, 128:256] = jnp.where(i0 == i1, 1.0, 0.0).astype(F32)
    factor_steps(d_ref, 0, 8)


def cholesky_second(b, a_ref, x_ref, d_ref):
    lo, hi = 128 * b, 128 * b + 128
    factor_steps(d_ref, 8, 16)
    xd = d_ref[:, 128:256]
    x_row = dot_nn(xd, x_ref[lo:hi, 0:hi])
    x_ref[lo:hi, 0:hi] = x_row
    if hi < PANEL:
        right = dot_nn(xd, a_ref[lo:hi, hi:PANEL])
        a_ref[hi:PANEL, hi:PANEL] = a_ref[hi:PANEL, hi:PANEL] - dot_tn(right, right)
        x_ref[hi:PANEL, 0:hi] = x_ref[hi:PANEL, 0:hi] - dot_tn(right, x_row)


def kernel(
    gen, rel, out, panel,
    sum_a, sum_b, scale_buf, rel_piece, own_rows, cols, top, top_a,
    early, part_e, recv_e, piece, a11, part_u, recv_u, a21, upper, amat, xmat, dmat, comb_t,
    local_sem, send_sem, recv_sem,
):
    x = lax.axis_index("snp")
    r = lax.axis_index("rows")
    y, z, c = r // 16, (r // 2) % 8, r % 2
    k_own = 2 * z + c
    count = [0]
    unsent = []

    def device(xx, yy, zz, cc):
        return (xx, yy * 16 + zz * 2 + cc)

    def x_peer(d):
        return device((x + d) % X, y, z, c)

    def y_peer(d):
        return device(x, (y + d) % Y, z, c)

    def z_peer(d):
        return device(x, y, (z + d) % Z, c)

    sibling = device(x, y, z, 1 - c)
    mirror = device(y, x, z, c)

    def slots(n):
        first = count[0]
        count[0] += n
        return first

    def describe(src, dst, to, slot):
        return pltpu.make_async_remote_copy(
            src_ref=src, dst_ref=dst, send_sem=send_sem.at[slot], recv_sem=recv_sem.at[slot],
            device_id=to, device_id_type=MESH,
        )

    def send(src, dst, to):
        copy = describe(src, dst, to, slots(1))
        copy.start()
        unsent.append((None, copy))
        return copy

    def send_if(cond, src, dst, to):
        copy = describe(src, dst, to, slots(1))
        pl.when(cond)(copy.start)
        unsent.append((cond, copy))
        return copy

    def arrive(copies):
        for copy in copies:
            copy.wait_recv()

    barrier = pltpu.get_barrier_semaphore()
    greeted = [x_peer(d) for d in range(1, X)]
    greeted += [device(x, (y + d) % Y, z, (c + e) % C) for d in range(Y) for e in range(C) if d or e]
    greeted += [z_peer(d) for d in range(1, Z)]
    for to in greeted:
        pl.semaphore_signal(barrier, inc=1, device_id=to, device_id_type=MESH)

    @pl.when(x != y)
    def _():
        pl.semaphore_signal(barrier, inc=1, device_id=mirror, device_id_type=MESH)

    values = gen[...]
    called = values >= 0
    dosage = jnp.where(called, values, 0.0)
    sums = jnp.concatenate(
        [jnp.sum(dosage, axis=0, keepdims=True), jnp.sum(called.astype(F32), axis=0, keepdims=True)], 0
    )
    yc = 2 * y + c
    sum_a[yc] = sums

    @pl.when(x != y)
    def _():
        pl.semaphore_wait(barrier, len(greeted) + 1)

    @pl.when(x == y)
    def _():
        pl.semaphore_wait(barrier, len(greeted))

    rel_copies = []
    rel_slot = slots(1)
    rel_send = slots(3)
    for d in range(1, X):
        copy = pltpu.make_async_remote_copy(
            src_ref=rel.at[:, 128 * d : 128 * d + 128], dst_ref=rel_piece,
            send_sem=send_sem.at[rel_send + d - 1], recv_sem=recv_sem.at[rel_slot],
            device_id=device(d, y, z, c), device_id_type=MESH,
        )
        rel_copies.append(copy)

    @pl.when(x == 0)
    def _():
        for copy in rel_copies:
            copy.start()
        local = pltpu.make_async_copy(rel.at[:, 0:128], rel_piece, local_sem)
        local.start()
        local.wait()

    for copy in rel_copies:
        unsent.append((x == 0, copy))

    copies = [
        send(sum_a.at[yc], sum_a.at[yc], device(x, (y + d) % Y, z, (c + e) % C))
        for d in range(Y) for e in range(C) if d or e
    ]
    arrive(copies)
    sum_b[z] = jnp.sum(sum_a[...], axis=0)
    copies = [send(sum_b.at[z], sum_b.at[z], z_peer(d)) for d in range(1, Z)]
    arrive(copies)
    both = jnp.sum(sum_b[...], axis=0)
    frequency = both[0:1, :] / (2.0 * both[1:2, :])
    scale_part = jnp.sum(2.0 * frequency * (1.0 - frequency))
    scale_buf[x] = jnp.full((8, 128), scale_part, F32)
    scale_copies = [send(scale_buf.at[x], scale_buf.at[x], x_peer(d)) for d in range(1, X)]
    own_rows[x] = jnp.where(called, dosage - 2.0 * frequency, 0.0).astype(BF16)

    def wait_if(cond, copies):
        @pl.when(cond)
        def _():
            for copy in copies:
                copy.wait_recv()

    wait_if(x != 0, rel_copies[:1])
    source = jnp.logical_and(y == 0, z < 2)
    own_slice = pl.ds(pl.multiple_of(k_own * IND, 16), IND)

    class Broadcast:
        def __init__(self, block, at, whole):
            self.at, self.whole = at, whole
            slot, first = slots(1), slots(Y - 1)
            self.quarters = [
                pltpu.make_async_remote_copy(
                    src_ref=block(q), dst_ref=at(k_own, q), send_sem=send_sem.at[first + q - 1],
                    recv_sem=recv_sem.at[slot], device_id=device(x, q, z, c), device_id_type=MESH,
                )
                for q in range(1, Y)
            ]

            @pl.when(source)
            def _():
                for copy in self.quarters:
                    copy.start()
                at(k_own, 0)[...] = block(0)[...]

            for copy in self.quarters:
                unsent.append((source, copy))

        def along_z(self):
            wait_if(jnp.logical_and(y != 0, z < 2), self.quarters[:1])
            self.slot, first = slots(2), slots(Z - 1)
            ref = self.at(k_own, y)
            copies = [
                pltpu.make_async_remote_copy(
                    src_ref=ref, dst_ref=ref, send_sem=send_sem.at[first + d - 1],
                    recv_sem=recv_sem.at[self.slot + z % 2], device_id=z_peer(d), device_id_type=MESH,
                )
                for d in range(1, Z)
            ]

            @pl.when(z < 2)
            def _():
                for copy in copies:
                    copy.start()

            for copy in copies:
                unsent.append((z < 2, copy))

        def along_y(self):
            refs = [self.at(2 * zs + c, y) for zs in range(2)]
            for zs in range(2):
                wait_if(z != zs, [describe(refs[zs], refs[zs], z_peer(1), self.slot + zs)])
            self.copies = [send(ref, ref, y_peer(d)) for d in range(1, Y) for ref in refs]

        def to_sibling(self):
            arrive(self.copies)
            refs = [self.whole(2 * zs + c) for zs in range(2)]
            self.copies = [send(ref, ref, sibling) for ref in refs]

        def finish(self):
            arrive(self.copies)

    def quarter(first, q):
        rows = pl.ds(pl.multiple_of(first + 80 * (q // 2), 16), 80)
        return rows, pl.ds(pl.multiple_of(384 * (q % 2), 128), 384)

    z_mate = device(x, y, z + 1 - 2 * (z % 2), c)
    early_copies = [send_if(source, own_rows.at[x], early.at[own_slice], z_mate)]
    top_cast = Broadcast(
        lambda q: own_rows.at[(x,) + quarter(0, q)],
        lambda k, q: top.at[quarter(k * IND, q)],
        lambda k: top.at[pl.ds(pl.multiple_of(k * IND, 16), IND)],
    )
    swap = send_if(x != y, own_rows.at[x], cols.at[x, own_slice], mirror)

    @pl.when(x == y)
    def _():
        cols[x, own_slice] = own_rows[x]

    @pl.when(source)
    def _():
        early[own_slice] = own_rows[x]

    top_cast.along_z()
    wait_if(source, early_copies)
    early_copies = []
    for zs in range(2):
        ref = early.at[pl.ds(pl.multiple_of((2 * zs + c) * IND, 16), IND)]
        early_copies.append(send_if(source, ref, ref, sibling))
    wait_if(source, early_copies)

    @pl.when(source)
    def _():
        for xx in range(X):
            part_e[xx] = dot_nt(own_rows[x], early[128 * xx : 128 * xx + 128, :])

    early_copies = [send_if(source, part_e.at[(x + d) % X], recv_e.at[d - 1], x_peer(d)) for d in range(1, X)]
    arrive(scale_copies)
    scale = 1.0 / (scale_buf[0] + scale_buf[1] + scale_buf[2] + scale_buf[3])[0:1, 0:1]

    def add_up(part, recv):
        lane = 128 * x + lax.broadcasted_iota(jnp.int32, (IND, 128), 1)
        row = IND * r + lax.broadcasted_iota(jnp.int32, (IND, 128), 0)
        total = part[x] + recv[0] + recv[1] + recv[2]
        return rel_piece[...] + total * scale + jnp.where(lane == row, RIDGE, 0.0)

    def part_rows(k, part, half):
        first, size = (0, 64) if part == 0 else (64, 96)
        if half is not None:
            first, size = first + size // 2 * half, size // 2
        return pl.ds(pl.multiple_of(k * IND + first, 16), size)

    def col_at(a, k, part, half=None):
        return cols.at[a, part_rows(k, part, half)]

    def up_at(a, k, part, half=None):
        return upper.at[a, part_rows(k, part, half)]

    class Gather:
        def __init__(self, at):
            self.at = at
            self.passed = {}
            self.across = [self.move(at(y, k_own, 0), y_peer(d)) for d in range(1, Y)]
            self.ring_two = [self.move(at(y, k_own, 1), z_peer(d)) for d in (1, Z - 1)]
            self.near = [(0, [k_own], self.fan([k_own]))]
            self.far = []

        def move(self, ref, to):
            return send(ref, ref, to)

        def fan(self, ks):
            return [self.move(self.at(y, k, 1), y_peer(d)) for k in ks for d in (1, Y - 1)]

        def at_distance(self, t):
            return 2 * ((z + Z - t) % Z) + c, 2 * ((z + t) % Z) + c

        def two(self, t):
            arrive(self.ring_two)
            plus, minus = self.at_distance(t)
            if t < 3:
                self.ring_two = [self.move(self.at(y, plus, 1), z_peer(1)), self.move(self.at(y, minus, 1), z_peer(Z - 1))]
            elif t == 3:
                self.ring_two = [
                    self.move(self.at(y, plus, 1, 0), z_peer(1)), self.move(self.at(y, minus, 1, 1), z_peer(Z - 1))
                ]
            ks = [plus, minus] if t < 4 else [plus]
            self.near.append((t, ks, self.fan(ks)))

        def one(self, t):
            if t == 0:
                arrive(self.across)
            plus, minus = self.at_distance(t)
            low, high = slice(0, 2), slice(2, 4)
            after = []
            for i, some in enumerate((low, high)):
                if t > 0:
                    arrive(self.ring_one[2 * i : 2 * i + 2])
                if t < 3:
                    after += [self.move(self.at(some, plus, 0), z_peer(1)), self.move(self.at(some, minus, 0), z_peer(Z - 1))]
                elif t == 3 and i == 0:
                    after.append(self.move(self.at(low, plus, 0), z_peer(1)))
                elif t == 3:
                    after.append(self.move(self.at(high, minus, 0), z_peer(Z - 1)))
            self.ring_one = after
            self.hand_on([plus, minus] if 0 < t < 4 else [plus], t, 0)

        def hop(self):
            t, ks, copies = self.near.pop(0)
            arrive(copies)
            made = []
            for k in ks:
                made.append(self.move(self.at((y + Y - 1) % Y, k, 1, 0), y_peer(1)))
                made.append(self.move(self.at((y + 1) % Y, k, 1, 1), y_peer(Y - 1)))
            self.far.append((t, ks, made))

        def pass_two(self):
            t, ks, copies = self.far.pop(0)
            arrive(copies)
            self.hand_on(ks, t, 1)

        def hand_on(self, ks, t, part):
            made = [self.move(self.at(slice(None), k, part), sibling) for k in ks]
            self.passed.setdefault(t, []).extend(made)

        def complete(self, t):
            arrive(self.passed[t])

        def finish(self):
            while self.near:
                self.hop()
                if len(self.far) > 1:
                    self.pass_two()
            while self.far:
                self.pass_two()

    wait_if(x != y, [swap])
    gather = Gather(col_at)
    row_copies = [send(own_rows.at[x], own_rows.at[x], x_peer(d)) for d in range(1, X)]
    wait_if(source, early_copies)

    @pl.when(source)
    def _():
        piece[...] = add_up(part_e, recv_e)

    a_cast = Broadcast(
        lambda q: piece.at[pl.ds(40 * q, 40)],
        lambda k, q: top_a.at[pl.ds(pl.multiple_of(k * IND + 40 * q, 8), 40)],
        lambda k: top_a.at[pl.ds(pl.multiple_of(k * IND, 8), IND)],
    )
    a_cast.along_z()
    top_cast.along_y()
    gather.two(1)
    gather.one(0)
    a_cast.along_y()
    gather.two(2)
    gather.hop()
    a_cast.to_sibling()
    a_cast.finish()
    half = pl.ds(pl.multiple_of(256 * c, 8), 256)
    a11[x, half] = top_a[half]
    a_copies = [send(a11.at[x, half], a11.at[x, half], x_peer(d)) for d in range(1, X)]
    top_cast.to_sibling()
    gather.two(3)
    gather.hop()
    gather.pass_two()
    top_cast.finish()

    for xx in range(X):
        part_u[xx] = dot_nt(own_rows[x], top[128 * xx : 128 * xx + 128, :])
    u_copies = [send(part_u.at[(x + d) % X], recv_u.at[d - 1], x_peer(d)) for d in range(1, X)]
    gather.one(1)
    arrive(a_copies)
    a_copy = send(a11.at[:, half], a11.at[:, half], sibling)
    gather.two(4)
    gather.hop()
    gather.pass_two()
    a_copy.wait_recv()
    for xx in range(X):
        amat[:, 128 * xx : 128 * xx + 128] = a11[xx]
    i0 = lax.broadcasted_iota(jnp.int32, (PANEL, PANEL), 0)
    i1 = lax.broadcasted_iota(jnp.int32, (PANEL, PANEL), 1)
    xmat[...] = jnp.where(i0 == i1, 1.0, 0.0).astype(F32)
    arrive(u_copies)
    mine = add_up(part_u, recv_u)
    a21[x] = mine
    u_swap = send_if(x != y, a21.at[x], upper.at[x, own_slice], mirror)

    @pl.when(x == y)
    def _():
        upper[x, own_slice] = mine

    u_copies = [send(a21.at[x], a21.at[x], x_peer(d)) for d in range(1, X)]
    cholesky_first(0, amat, dmat)
    gather.one(2)
    gather.hop()
    gather.pass_two()
    wait_if(x != y, [u_swap])
    u_gather = Gather(up_at)
    cholesky_second(0, amat, xmat, dmat)
    gather.hop()
    gather.pass_two()
    u_gather.two(1)
    u_gather.one(0)
    cholesky_first(1, amat, dmat)
    gather.one(3)
    gather.pass_two()
    u_gather.two(2)
    u_gather.hop()
    cholesky_second(1, amat, xmat, dmat)
    u_gather.two(3)
    u_gather.hop()
    u_gather.one(1)
    cholesky_first(2, amat, dmat)
    gather.one(4)
    u_gather.pass_two()
    u_gather.two(4)
    u_gather.hop()
    arrive(row_copies)

    def chips(t):
        return [(z + Z - t) % Z, (z + t) % Z] if 0 < t < 4 else [(z + t) % Z]

    def gram_part(t):
        gather.complete(t)
        for chip in chips(t):
            rows = pl.ds(pl.multiple_of(chip * 320, 16), 320)
            total = dot_nt(cols[0, rows], own_rows[0])
            for a in range(1, X):
                total = total + dot_nt(cols[a, rows], own_rows[a])
            comb_t[rows, :] = total * scale

    gram_part(0)
    cholesky_second(2, amat, xmat, dmat)
    u_gather.one(2)
    u_gather.pass_two()
    u_gather.hop()
    gram_part(1)
    cholesky_first(3, amat, dmat)
    u_gather.one(3)
    u_gather.pass_two()
    u_gather.hop()
    gram_part(2)
    cholesky_second(3, amat, xmat, dmat)
    u_gather.one(4)
    u_gather.pass_two()
    gather.finish()
    u_gather.finish()
    arrive(u_copies)
    own = jnp.concatenate([a21[0], a21[1], a21[2], a21[3]], 1)
    own_panel = dot_nt(own, xmat[...], HIGH)
    panel[...] = own_panel
    weights = dot_nn(own_panel, xmat[...])
    w_high = weights.astype(BF16)
    w_low = (weights - w_high.astype(F32)).astype(BF16)
    gram_part(3)
    gram_part(4)
    for t in range(5):
        u_gather.complete(t)
        for chip in chips(t):
            rows = pl.ds(pl.multiple_of(chip * 320, 16), 320)
            up = jnp.concatenate([upper[0, rows], upper[1, rows], upper[2, rows], upper[3, rows]], 1)
            up_high = up.astype(BF16)
            up_low = (up - up_high.astype(F32)).astype(BF16)
            prod = dot_nt(up_low, w_high) + dot_nt(up_high, w_low) + dot_nt(up_high, w_high)
            comb_t[rows, :] = comb_t[rows, :] - prod
    for i in range(WIDTH // 128):
        lanes = slice(128 * i, 128 * i + 128)
        out[:, lanes] = comb_t[lanes, :].T

    for cond, copy in unsent:
        if cond is None:
            copy.wait_send()
        else:
            pl.when(cond)(copy.wait_send)
    assert count[0] <= COPIES, count[0]


def per_device(genotypes, relationship):
    vmem = pl.BlockSpec(memory_space=pltpu.VMEM)
    added, own_panel = pl.pallas_call(
        kernel,
        out_shape=(
            jax.ShapeDtypeStruct((IND, WIDTH), F32),
            jax.ShapeDtypeStruct((IND, PANEL), F32),
        ),
        in_specs=[vmem, pl.BlockSpec(memory_space=pl.ANY)],
        out_specs=(vmem, vmem),
        scratch_shapes=[
            pltpu.VMEM((8, 2, SNP), F32),
            pltpu.VMEM((8, 2, SNP), F32),
            pltpu.VMEM((X, 8, 128), F32),
            pltpu.VMEM((IND, 128), F32),
            pltpu.VMEM((X, IND, SNP), BF16),
            pltpu.VMEM((X, WIDTH, SNP), BF16),
            pltpu.VMEM((640, SNP), BF16),
            pltpu.VMEM((640, 128), F32),
            pltpu.VMEM((640, SNP), BF16),
            pltpu.VMEM((X, IND, 128), F32),
            pltpu.VMEM((3, IND, 128), F32),
            pltpu.VMEM((IND, 128), F32),
            pltpu.VMEM((X, PANEL, 128), F32),
            pltpu.VMEM((X, IND, 128), F32),
            pltpu.VMEM((3, IND, 128), F32),
            pltpu.VMEM((X, IND, 128), F32),
            pltpu.VMEM((X, WIDTH, 128), F32),
            pltpu.VMEM((PANEL, PANEL), F32),
            pltpu.VMEM((PANEL, PANEL), F32),
            pltpu.VMEM((128, 256), F32),
            pltpu.VMEM((WIDTH, IND), F32),
            pltpu.SemaphoreType.DMA,
            pltpu.SemaphoreType.DMA((COPIES,)),
            pltpu.SemaphoreType.DMA((COPIES,)),
        ],
        compiler_params=pltpu.CompilerParams(
            collective_id=0, has_side_effects=True, vmem_limit_bytes=56 * 1024 * 1024
        ),
        name="update",
    )(genotypes.T, relationship)
    row = IND * lax.axis_index("rows") + lax.broadcasted_iota(jnp.int32, (IND, WIDTH), 0)
    col = WIDTH * lax.axis_index("snp") + lax.broadcasted_iota(jnp.int32, (IND, WIDTH), 1)
    return relationship + added + jnp.where(row == col, RIDGE, 0.0), own_panel


def solution(mesh):
    return jax.shard_map(
        per_device,
        mesh=mesh,
        in_specs=(P("snp", "rows"), P("rows", "snp")),
        out_specs=(P("rows", "snp"), P("rows", None)),
        check_vma=False,
    )
```

time: 159 us -> 138 us (0.87); the launches traced: 159 us -> 135 us
  Pallas kernels: 155 us -> 131 us
  other arithmetic: 0 us -> 2.96 us
  local copies, waits for them, and re-layouts: 3.48 us -> 0.73 us
    pallas_call x1, Pallas kernels: 155 us -> 131 us  [per_device(): pl.pallas_call(kernel, out_shape=(jax.ShapeDtypeStruct((IND, WIDTH), F32)...]
    add x0 -> x3, other arithmetic: none -> 2.96 us  [the longest x1 2.95 us: per_device(): return (relationship + added + jnp.where(row == col, RIDGE, 0.0), own_panel)]
    unnamed x4 -> x5, local copies, waits for them, and re-layouts: 3.48 us -> 0.73 us
where the time goes in v2:
time: 138 us; the launch traced here: 135 us
  Pallas kernels  131 us (95%)
  other arithmetic  2.96 us (2%)
    pallas_call x1, Pallas kernels, per_device(): pl.pallas_call(kernel, out_shape=(jax.ShapeDtypeStruct((IND, WIDTH), F32)...  131 us
    add x1, other arithmetic, per_device(): return (relationship + added + jnp.where(row == col, RIDGE, 0.0), own_panel)  2.95 us

profile of v2, /device:TPU:1, one launch (start us, length us, event | category | flops | bytes accessed | tf_op | source)
XLA Modules:
  0.0 135.2 jit_solution(13616884185627169703)
XLA Ops:
  0.6 0.0 copy-start
  0.7 130.8 %update.1 = (f32[160,2560]{1,0:T(8,128)}, f32[160,512]{1,0:T(8,128)}) custom-call(f32[160,768]{1,0:T(8,128)} %bitcast.1, f32[160,2560]{1,0:T(8,128)} %rel.1), custom_call_target="tpu_custom_call" | custom-call | tf_op jit(solution)/shard_map/update/pallas_call | solution.py:559
  131.5 0.0 copy-done
  131.5 0.0 copy-start.1
  131.5 2.9 %select_add_fusion = f32[160,2560]{1,0:T(8,128)} fusion(f32[160,2560]{1,0:T(8,128)S(1)} %copy-done, f32[160,2560]{1,0:T(8,128)} %get-tuple-element.4, s32[2560]{0:T(1024)S(1)} %iota_add_fusion, s32[160]{0:T(256)S(1)} %iota_add_fusion.1), kind=kLoop, calls=%fused_computation | loop fusion | flops 1638400 | bytes 4926080 | tf_op jit(solution)/shard_map/add | solution.py:600
  134.5 0.0 copy-done.1
  134.5 0.7 copy.5
  (2 shorter events, 0.0 us)
Async XLA Ops:
  0.6 130.9 %copy-start = (f32[160,2560]{1,0:T(8,128)S(1)}, f32[160,2560]{1,0:T(8,128)}, u32[]{:S(2)}) copy-start(f32[160,2560]{1,0:T(8,128)} %rel.1) | copy-start | bytes 4915204
  131.5 3.0 %copy-start.1 = (f32[160,512]{1,0:T(8,128)S(1)}, f32[160,512]{1,0:T(8,128)}, u32[]{:S(2)}) copy-start(f32[160,512]{1,0:T(8,128)} %get-tuple-element.9) | copy-start | bytes 983044

commit v3 on v2

--- a/solution.py
+++ b/solution.py
@@ -430,51 +430,61 @@
     top_cast.along_y()
     gather.two(1)
     gather.one(0)
+    top_cast.to_sibling()
     a_cast.along_y()
     gather.two(2)
     gather.hop()
+    top_cast.finish()
+
+    for xx in range(X):
+        part_u[xx] = dot_nt(own_rows[x], top[128 * xx : 128 * xx + 128, :])
+    u_copies = [send(part_u.at[(x + d) % X], recv_u.at[d - 1], x_peer(d)) for d in range(1, X)]
     a_cast.to_sibling()
     a_cast.finish()
     half = pl.ds(pl.multiple_of(256 * c, 8), 256)
     a11[x, half] = top_a[half]
     a_copies = [send(a11.at[x, half], a11.at[x, half], x_peer(d)) for d in range(1, X)]
-    top_cast.to_sibling()
     gather.two(3)
     gather.hop()
-    gather.pass_two()
-    top_cast.finish()
-
-    for xx in range(X):
-        part_u[xx] = dot_nt(own_rows[x], top[128 * xx : 128 * xx + 128, :])
-    u_copies = [send(part_u.at[(x + d) % X], recv_u.at[d - 1], x_peer(d)) for d in range(1, X)]
-    gather.one(1)
+    arrive(u_copies)
+    mine = add_up(part_u, recv_u)
+    a21[x] = mine
+    u_swap = send_if(x != y, a21.at[x], upper.at[x, own_slice], mirror)
+
+    @pl.when(x == y)
+    def _():
+        upper[x, own_slice] = mine
+
+    u_copies = [send(a21.at[x], a21.at[x], x_peer(d)) for d in range(1, X)]
     arrive(a_copies)
     a_copy = send(a11.at[:, half], a11.at[:, half], sibling)
+    gather.one(1)
     gather.two(4)
     gather.hop()
-    gather.pass_two()
+    wait_if(x != y, [u_swap])
+    u_gather = Gather(up_at)
     a_copy.wait_recv()
     for xx in range(X):
         amat[:, 128 * xx : 128 * xx + 128] = a11[xx]
     i0 = lax.broadcasted_iota(jnp.int32, (PANEL, PANEL), 0)
     i1 = lax.broadcasted_iota(jnp.int32, (PANEL, PANEL), 1)
     xmat[...] = jnp.where(i0 == i1, 1.0, 0.0).astype(F32)
-    arrive(u_copies)
-    mine = add_up(part_u, recv_u)
-    a21[x] = mine
-    u_swap = send_if(x != y, a21.at[x], upper.at[x, own_slice], mirror)
-
-    @pl.when(x == y)
-    def _():
-        upper[x, own_slice] = mine
-
-    u_copies = [send(a21.at[x], a21.at[x], x_peer(d)) for d in range(1, X)]
+    def chips(t):
+        return [(z + Z - t) % Z, (z + t) % Z] if 0 < t < 4 else [(z + t) % Z]
+
+    def gram_part(t):
+        gather.complete(t)
+        for chip in chips(t):
+            rows = pl.ds(pl.multiple_of(chip * 320, 16), 320)
+            total = dot_nt(cols[0, rows], own_rows[0])
+            for a in range(1, X):
+                total = total + dot_nt(cols[a, rows], own_rows[a])
+            comb_t[rows, :] = total * scale
+
     cholesky_first(0, amat, dmat)
     gather.one(2)
     gather.hop()
     gather.pass_two()
-    wait_if(x != y, [u_swap])
-    u_gather = Gather(up_at)
     cholesky_second(0, amat, xmat, dmat)
     gather.hop()
     gather.pass_two()
@@ -486,28 +496,16 @@
     u_gather.two(2)
     u_gather.hop()
     cholesky_second(1, amat, xmat, dmat)
+    gather.pass_two()
     u_gather.two(3)
     u_gather.hop()
     u_gather.one(1)
     cholesky_first(2, amat, dmat)
     gather.one(4)
-    u_gather.pass_two()
+    gather.pass_two()
     u_gather.two(4)
     u_gather.hop()
     arrive(row_copies)
-
-    def chips(t):
-        return [(z + Z - t) % Z, (z + t) % Z] if 0 < t < 4 else [(z + t) % Z]
-
-    def gram_part(t):
-        gather.complete(t)
-        for chip in chips(t):
-            rows = pl.ds(pl.multiple_of(chip * 320, 16), 320)
-            total = dot_nt(cols[0, rows], own_rows[0])
-            for a in range(1, X):
-                total = total + dot_nt(cols[a, rows], own_rows[a])
-            comb_t[rows, :] = total * scale
-
     gram_part(0)
     cholesky_second(2, amat, xmat, dmat)
     u_gather.one(2)
@@ -516,6 +514,7 @@
     gram_part(1)
     cholesky_first(3, amat, dmat)
     u_gather.one(3)
+    u_gather.pass_two()
     u_gather.pass_two()
     u_gather.hop()
     gram_part(2)
@@ -544,7 +543,9 @@
             comb_t[rows, :] = comb_t[rows, :] - prod
     for i in range(WIDTH // 128):
         lanes = slice(128 * i, 128 * i + 128)
-        out[:, lanes] = comb_t[lanes, :].T
+        lane = WIDTH * x + 128 * i + lax.broadcasted_iota(jnp.int32, (IND, 128), 1)
+        row = IND * r + lax.broadcasted_iota(jnp.int32, (IND, 128), 0)
+        out[:, lanes] = comb_t[lanes, :].T + jnp.where(lane == row, RIDGE, 0.0)
 
     for cond, copy in unsent:
         if cond is None:
@@ -595,9 +596,7 @@
         ),
         name="update",
     )(genotypes.T, relationship)
-    row = IND * lax.axis_index("rows") + lax.broadcasted_iota(jnp.int32, (IND, WIDTH), 0)
-    col = WIDTH * lax.axis_index("snp") + lax.broadcasted_iota(jnp.int32, (IND, WIDTH), 1)
-    return relationship + added + jnp.where(row == col, RIDGE, 0.0), own_panel
+    return relationship + added, own_panel
 
 
 def solution(mesh):

time: 138 us -> 135 us (0.978)
  Pallas kernels: 131 us -> 128 us
    pallas_call x1, Pallas kernels: 131 us -> 128 us  [per_device(): pl.pallas_call(kernel, out_shape=(jax.ShapeDtypeStruct((IND, WIDTH), F32)...]
    add x3 -> x1, other arithmetic: 2.96 us -> 2.81 us  [per_device(): return (relationship + added, own_panel)]
where the time goes in v3:
time: 135 us; the launch traced here: 133 us
  Pallas kernels  128 us (95%)
  other arithmetic  2.81 us (2%)
    pallas_call x1, Pallas kernels, per_device(): pl.pallas_call(kernel, out_shape=(jax.ShapeDtypeStruct((IND, WIDTH), F32)...  128 us
    add x1, other arithmetic, per_device(): return (relationship + added, own_panel)  2.81 us

profile of v3, /device:TPU:1, one launch (start us, length us, event | category | flops | bytes accessed | tf_op | source)
XLA Modules:
  0.0 132.6 jit_solution(11363149834900536547)
XLA Ops:
  0.6 0.0 copy-start
  0.6 128.4 %update.1 = (f32[160,2560]{1,0:T(8,128)}, f32[160,512]{1,0:T(8,128)}) custom-call(f32[160,768]{1,0:T(8,128)} %bitcast.1, f32[160,2560]{1,0:T(8,128)} %rel.1), custom_call_target="tpu_custom_call" | custom-call | tf_op jit(solution)/shard_map/update/pallas_call | solution.py:560
  129.0 0.0 copy-done
  129.1 0.0 copy-start.1
  129.1 2.8 %add.3 = f32[160,2560]{1,0:T(8,128)} add(f32[160,2560]{1,0:T(8,128)S(1)} %copy-done, f32[160,2560]{1,0:T(8,128)} %get-tuple-element.4) | non-fusion elementwise | flops 409600 | bytes 4915200 | tf_op jit(solution)/shard_map/add | solution.py:599
  131.9 0.0 copy-done.1
  131.9 0.7 copy.5
Async XLA Ops:
  0.6 128.4 %copy-start = (f32[160,2560]{1,0:T(8,128)S(1)}, f32[160,2560]{1,0:T(8,128)}, u32[]{:S(2)}) copy-start(f32[160,2560]{1,0:T(8,128)} %rel.1) | copy-start | bytes 4915204
  129.1 2.8 %copy-start.1 = (f32[160,512]{1,0:T(8,128)S(1)}, f32[160,512]{1,0:T(8,128)}, u32[]{:S(2)}) copy-start(f32[160,512]{1,0:T(8,128)} %get-tuple-element.9) | copy-start | bytes 983044
